TPU v7x, 256 devices: a whole 4x4x8 slice. The times are simulated.
256 devices in a mesh: paper: 64 (over z, y, core), author: 4 (over x).
Axes of the slice: x: 4, y: 4, z: 8, core: 2. Of those that a mesh axis runs over, the one named last changes fastest.
Arguments:
- paper_feat: bfloat16 [16384, 1024], P('paper', 'author'), may hold values from -6 to 6
- author_feat: bfloat16 [16384, 1024], P('paper', 'author'), may hold values from -6 to 6
- cite_owner: int32 [3072, 1], P('paper'), may hold values from 0 to 63; in each aligned block of 48 rows (0 to 47, 48 to 95, ...) no two rows name the same one
- cite_source: int32 [3072], P('paper'), may hold values from 0 to 1
- cite_target: int32 [3072], P('paper'), may hold values from 0 to 1
- cite_edges: int32 [3072], P('paper'), may hold values from 8 to 64
- cite_count: int32 [64], P('paper'), may hold values from 36 to 48, as said below
- citation_weight_tiles: bfloat16 [3072, 128, 128], P('paper'), may hold values from 0 to 1
- write_owner: int32 [2048, 1], P('paper'), may hold values from 0 to 63; in each aligned block of 32 rows (0 to 31, 32 to 63, ...) no two rows name the same one
- write_paper: int32 [2048], P('paper'), may hold values from 0 to 1
- write_author: int32 [2048], P('paper'), may hold values from 0 to 1
- write_edges: int32 [2048], P('paper'), may hold values from 8 to 64
- authorship_weight_tiles: bfloat16 [2048, 128, 128], P('paper'), may hold values from 0 to 1
- w_self: bfloat16 [1024, 1024], replicated, may hold values from -0.1875 to 0.1875
- w_cite: bfloat16 [1024, 1024], replicated, may hold values from -0.1875 to 0.1875
- w_write: bfloat16 [1024, 1024], replicated, may hold values from -0.1875 to 0.1875
- cotangent: bfloat16 [16384, 1024], P('paper', 'author'), may hold values from -6 to 6
Outputs:
- paper_out: bfloat16 [16384, 1024], P('paper', 'author')
- paper_grad: bfloat16 [16384, 1024], P('paper', 'author')
- author_grad: bfloat16 [16384, 1024], P('paper', 'author')
Inputs may be any that keep to these rules, and one draw needn't show every extreme that they name: `cite_owner`: among the 48 tiles of one paper index (live or not), at most 1 have their source on any one paper index. The live tiles of a paper index are the first cite_count of its list; some paper index has all 48 live. `write_owner`: among the 32 tiles of one paper index, at most 1 take their author block from any one paper index.
All inputs are finite; a program needn't handle non-finite values.
Results may differ from a plain program's by a relative error of at most 0.007.
Values may be sent and summed in bfloat16 or wider, within the bound.
A program may use at most 128 MiB of HBM per device.

v0:
```python
import jax
import jax.numpy as jnp
from jax import lax
from jax.sharding import PartitionSpec as P

TOP_PRECISION = lax.Precision.HIGHEST


def silu_slope(values):
    sigma = jax.nn.sigmoid(values)
    return sigma * (1.0 + values * (1.0 - sigma))


def matmul(left, right):
    return jnp.dot(left, right, preferred_element_type=jnp.float32)


def matmul_flipped(left, right):
    return lax.dot_general(
        left, right, (((1,), (1,)), ((), ())), preferred_element_type=jnp.float32
    )


def slot_layout(owners, slot_count, slot_total):
    count = owners.shape[0]
    order = jnp.arange(count, dtype=jnp.int32)
    earlier = (owners[:, None] == owners[None, :]) & (order[:, None] > order[None, :])
    rank = jnp.sum(earlier.astype(jnp.int32), axis=1)
    position = owners * slot_count + rank
    positioned_rows = position[:, None] == jnp.arange(slot_total, dtype=jnp.int32)[None, :]
    return (position, positioned_rows)


def body(
    paper_feat,
    author_feat,
    cite_owner,
    cite_source,
    cite_target,
    cite_edges,
    cite_count,
    citation_weight_tiles,
    write_owner,
    write_paper,
    write_author,
    write_edges,
    authorship_weight_tiles,
    w_self,
    w_cite,
    w_write,
    cotangent,
):
    peer_count = lax.axis_size("paper")
    tile_total = citation_weight_tiles.shape[0]
    tile_rows = citation_weight_tiles.shape[1]
    paper_rows, quarter = paper_feat.shape
    author_rows = author_feat.shape[0]
    paper_blocks = paper_rows // tile_rows
    author_blocks = author_rows // tile_rows
    slot_count = tile_total // peer_count + 1
    slot_total = peer_count * slot_count
    write_total = authorship_weight_tiles.shape[0]
    wslot_count = write_total // peer_count + 1
    wslot_total = peer_count * wslot_count
    block_range = jnp.arange(paper_blocks, dtype=jnp.int32)
    author_range = jnp.arange(author_blocks, dtype=jnp.int32)
    position, positioned_rows = slot_layout(cite_owner[:, 0], slot_count, slot_total)
    tile_order = jnp.arange(tile_total, dtype=jnp.int32)
    wanted = jnp.sum(jnp.where(positioned_rows, cite_source[:, None], 0), axis=0)
    incoming_ids = lax.all_to_all(
        wanted.reshape(peer_count, slot_count), "paper", split_axis=0, concat_axis=0, tiled=True
    )
    live_tile = tile_order < cite_count[0]
    tile_scale = jnp.where(live_tile, 1.0 / cite_edges.astype(jnp.float32), 0.0)
    target_hot = jnp.where(cite_target[:, None] == block_range[None, :], tile_scale[:, None], 0.0)
    slotted_weight_tiles = jnp.einsum(
        "tk,tab->kab",
        positioned_rows.astype(jnp.bfloat16),
        citation_weight_tiles,
        preferred_element_type=jnp.float32,
    ).astype(jnp.bfloat16)
    slotted_target_index = jnp.einsum(
        "tk,tp->kp", positioned_rows.astype(jnp.float32), target_hot, precision=TOP_PRECISION
    )
    pieces = lax.all_gather(paper_feat, "paper", axis=0, tiled=True)
    shard_count = pieces.shape[0] // paper_rows
    span = shard_count * slot_count
    shard_of = jnp.arange(span, dtype=jnp.int32) // slot_count
    stacked = pieces.reshape(shard_count * paper_blocks, tile_rows, quarter)
    selected_rows = jnp.take(stacked, shard_of * paper_blocks + wanted, axis=0)
    partial_block_value = jnp.einsum(
        "eih,ehp->eip", slotted_weight_tiles, selected_rows, preferred_element_type=jnp.float32
    )
    citation_accumulator = jnp.einsum(
        "nr,nmh->rmh", slotted_target_index, partial_block_value, precision=TOP_PRECISION
    )
    cite_sum = citation_accumulator.reshape(paper_rows, quarter).astype(jnp.bfloat16)
    wposition, wplaced = slot_layout(write_owner[:, 0], wslot_count, wslot_total)
    wanted_authors = jnp.sum(jnp.where(wplaced, write_author[:, None], 0), axis=0)
    author_ids = lax.all_to_all(
        wanted_authors.reshape(peer_count, wslot_count),
        "paper",
        split_axis=0,
        concat_axis=0,
        tiled=True,
    )
    author_stack = author_feat.reshape(author_blocks, tile_rows, quarter)
    author_out = jnp.take(author_stack, author_ids.reshape(-1), axis=0).reshape(
        peer_count, wslot_count, tile_rows, quarter
    )
    author_in = lax.all_to_all(author_out, "paper", split_axis=0, concat_axis=0, tiled=True)
    write_scale = 1.0 / write_edges.astype(jnp.float32)
    authorship_sources = jnp.take(
        author_in.reshape(wslot_total, tile_rows, quarter), wposition, axis=0
    )
    authorship_products = jnp.einsum(
        "eih,ehp->eip",
        authorship_weight_tiles,
        authorship_sources,
        preferred_element_type=jnp.float32,
    )
    paper_onehot_mask = jnp.where(
        write_paper[:, None] == block_range[None, :], write_scale[:, None], 0.0
    )
    authorship_sum = jnp.einsum(
        "nr,nmh->rmh", paper_onehot_mask, authorship_products, precision=TOP_PRECISION
    )
    authorship_sum = authorship_sum.reshape(paper_rows, quarter).astype(jnp.bfloat16)
    column = lax.axis_index("author") * quarter
    feats = lax.all_gather(paper_feat, "author", axis=1, tiled=True)
    cites = lax.all_gather(cite_sum, "author", axis=1, tiled=True)
    writes = lax.all_gather(authorship_sum, "author", axis=1, tiled=True)
    span = feats.shape[1]

    def window(weight):
        return lax.dynamic_slice(weight, (0, column), (span, quarter))

    preact = (
        matmul(feats, window(w_self))
        + matmul(cites, window(w_cite))
        + matmul(writes, window(w_write))
    )
    paper_out = (paper_feat.astype(jnp.float32) + jax.nn.silu(preact)).astype(jnp.bfloat16)
    grad_pre = (cotangent.astype(jnp.float32) * silu_slope(preact)).astype(jnp.bfloat16)
    pieces = lax.all_gather(grad_pre, "author", axis=1, tiled=True)
    fold_span = pieces.shape[1]

    def flipped(weight):
        return matmul_flipped(pieces, lax.dynamic_slice(weight, (column, 0), (quarter, fold_span)))

    self_back = flipped(w_self)
    cite_back = flipped(w_cite)
    write_back = flipped(w_write)
    cite_grad = cite_back.astype(jnp.bfloat16).reshape(paper_blocks, tile_rows, quarter)
    target_indices = jnp.take(cite_grad, cite_target, axis=0)
    returned_rows = jnp.einsum(
        "pdg,pdw->pgw", citation_weight_tiles, target_indices, preferred_element_type=jnp.float32
    )
    returned_rows = (returned_rows * tile_scale[:, None, None]).astype(jnp.bfloat16)
    outgoing_grad = jnp.einsum(
        "hs,hip->sip",
        positioned_rows.astype(jnp.bfloat16),
        returned_rows,
        preferred_element_type=jnp.float32,
    )
    outgoing_grad = outgoing_grad.astype(jnp.bfloat16).reshape(
        peer_count, slot_count, tile_rows, quarter
    )
    arrived = lax.all_to_all(outgoing_grad, "paper", split_axis=0, concat_axis=0, tiled=True)
    arrived_hot = (incoming_ids.reshape(-1)[:, None] == block_range[None, :]).astype(jnp.bfloat16)
    cite_return = jnp.einsum(
        "kp,kac->pac",
        arrived_hot,
        arrived.reshape(slot_total, tile_rows, quarter),
        preferred_element_type=jnp.float32,
    )
    paper_grad = (
        cotangent.astype(jnp.float32) + self_back + cite_return.reshape(paper_rows, quarter)
    ).astype(jnp.bfloat16)
    write_grad = write_back.astype(jnp.bfloat16).reshape(paper_blocks, tile_rows, quarter)
    authorship_targets = jnp.take(write_grad, write_paper, axis=0)
    author_products = jnp.einsum(
        "pdg,pdw->pgw",
        authorship_weight_tiles,
        authorship_targets,
        preferred_element_type=jnp.float32,
    )
    author_products = (author_products * write_scale[:, None, None]).astype(jnp.bfloat16)
    author_send = jnp.einsum(
        "hs,hip->sip",
        wplaced.astype(jnp.bfloat16),
        author_products,
        preferred_element_type=jnp.float32,
    )
    author_send = author_send.astype(jnp.bfloat16).reshape(
        peer_count, wslot_count, tile_rows, quarter
    )
    author_back = lax.all_to_all(author_send, "paper", split_axis=0, concat_axis=0, tiled=True)
    author_hot = (author_ids.reshape(-1)[:, None] == author_range[None, :]).astype(jnp.bfloat16)
    author_grad = jnp.einsum(
        "kp,kac->pac",
        author_hot,
        author_back.reshape(wslot_total, tile_rows, quarter),
        preferred_element_type=jnp.float32,
    )
    author_grad = author_grad.reshape(author_rows, quarter).astype(jnp.bfloat16)
    return (paper_out, paper_grad, author_grad)


def solution(mesh):
    in_specs = (
        P("paper", "author"),
        P("paper", "author"),
        P("paper", None),
        P("paper"),
        P("paper"),
        P("paper"),
        P("paper"),
        P("paper", None, None),
        P("paper", None),
        P("paper"),
        P("paper"),
        P("paper"),
        P("paper", None, None),
        P(),
        P(),
        P(),
        P("paper", "author"),
    )
    out_specs = (P("paper", "author"), P("paper", "author"), P("paper", "author"))
    return jax.shard_map(body, mesh=mesh, in_specs=in_specs, out_specs=out_specs, check_vma=False)
```

profile of v0, /device:TPU:2, one launch (start us, length us, event | category | flops | bytes accessed | tf_op | source)
XLA Modules:
  0.0 490.8 jit_solution(11593306411064109347)
XLA Ops:
  7.2 0.0 copy-start
  7.2 0.0 all-gather.2.cloned.1.call-start
  7.2 0.7 all-gather.2.cloned.1.call-update
  7.9 0.9 convert_reduce_fusion.1
  8.8 0.7 fusion.83
  9.5 0.7 select_reduce_fusion.1
  10.3 0.1 copy.96
  10.3 21.5 %all_to_all.39 = s32[64,1,1]{2,1,0:T(1,128)S(1)} all-to-all(s32[64,1,1]{2,1,0:T(1,128)S(1)} %copy.96), channel_id=1, replica_groups=mesh['paper'=64,'author'=4] {'paper'}, dimensions={0} | all-to-all | bytes 512 | tf_op jit(solution)/shard_map/all_to_all | solution.py:100
  31.8 1.2 reduce
  33.1 2.7 gather_fusion.1
  35.9 4.6 bitcast_select_fusion
  40.4 0.0 copy-start.10
  40.5 0.0 copy-start.14
  40.5 5.8 %all-to-all-start.1 = ((bf16[64,1,128,256]{3,2,1,0:T(8,128)(2,1)}), bf16[64,1,128,256]{3,2,1,0:T(8,128)(2,1)}, u32[]{:S(2)}, u32[]{:S(2)}) async-start(bf16[64,1,128,256]{3,2,1,0:T(8,128)(2,1)} %bitcast_select_fusion), calls=%async_computation.1 | async-start | bytes 8388608 | tf_op jit(solution)/shard_map/all_to_all | solution.py:111
  46.3 0.1 copy.90
  47.1 0.1 copy.101
  47.2 0.2 convert_reduce_fusion
  47.4 0.1 select_reduce_fusion
  47.5 0.7 copy.103
  48.3 0.3 convolution_bitcast_fusion.2
  48.6 0.2 copy-done.16
  48.8 13.0 %all_gather.15 = bf16[256,1024]{1,0:T(8,128)(2,1)S(1)} all-gather(bf16[256,256]{1,0:T(8,128)(2,1)S(1)} %copy-done.2), channel_id=1, replica_groups=mesh['paper'=64,'author'=4] {'author'}, dimensions={1}, use_global_device_ids=true | all-gather | bytes 655360 | tf_op jit(solution)/shard_map/all_gather | solution.py:130
  61.9 0.5 compare_and_fusion.1
  62.4 4.2 convolution_convert_fusion
  66.6 96.0 %all-to-all-done.1 = bf16[64,1,128,256]{3,2,1,0:T(8,128)(2,1)} async-done(((bf16[64,1,128,256]{3,2,1,0:T(8,128)(2,1)}), bf16[64,1,128,256]{3,2,1,0:T(8,128)(2,1)}, u32[]{:S(2)}, u32[]{:S(2)}) %all-to-all-start.1) | async-done | bytes 4194336 | tf_op jit(solution)/shard_map/all_to_all | solution.py:111
  162.6 5.4 %all-to-all-start.2 = ((s32[64,1,1]{2,1,0:T(1,128)}), s32[64,1,1]{2,1,0:T(1,128)}, u32[]{:S(2)}, u32[]{:S(2)}) async-start(s32[64,1,1]{2,1,0:T(1,128)} %copy.103), calls=%async_computation.2 | async-start | bytes 65536 | tf_op jit(solution)/shard_map/all_to_all | solution.py:70
  168.1 4.2 gather_fusion.2
  172.3 4.6 convolution_bitcast_fusion
  176.9 5.5 %copy.98 = f32[32,128,256]{2,0,1:T(8,128)} copy(f32[32,128,256]{1,2,0:T(8,128)} %convolution_bitcast_fusion) | data formatting | bytes 8388608 | tf_op jit(solution)/shard_map/eih,ehp->eip/dot_general | solution.py:116
  182.4 4.3 convolution_convert_fusion.3
  186.7 13.9 %all_gather.18 = bf16[256,1024]{1,0:T(8,128)(2,1)S(1)} all-gather(bf16[256,256]{1,0:T(8,128)(2,1)S(1)} %bitcast.106), channel_id=1, replica_groups=mesh['paper'=64,'author'=4] {'author'}, dimensions={1}, use_global_device_ids=true | all-gather | bytes 655360 | tf_op jit(solution)/shard_map/all_gather | solution.py:132
  200.6 6.2 %gather_fusion = bf16[64,128,256]{2,1,0:T(8,128)(2,1)} fusion(bf16[128,128,256]{2,1,0:T(8,128)(2,1)} %bitcast.104, s32[1024]{0:T(1024)S(1)} %pad_clamp_fusion.4), kind=kCustom, calls=%fused_computation | custom fusion | bytes 8388864 | tf_op jit(solution)/shard_map/jit(_take)/gather | solution.py:90
  206.8 5.1 %fusion.5 = f32[64,128,256]{2,1,0:T(8,128)S(1)} fusion(bf16[64,128,256]{2,1,0:T(8,128)(2,1)} %gather_fusion, pred[64]{0:T(512)(128)(4,1)S(1)} %compare_and_fusion.3, bf16[64,128,128]{2,0,1:T(8,128)(2,1)} %convolution_convert_fusion), kind=kOutput, calls=%fused_computation.15 | convolution fusion | flops 538968064 | bytes 14680128 | tf_op jit(solution)/shard_map/eih,ehp->eip/dot_general | solution.py:91
  211.9 8.6 %fusion.31 = bf16[2,128,256]{2,0,1:T(2,128)(2,1)S(1)} fusion(f32[64,2,1]{0,1,2:T(2,128)S(1)} %convolution_bitcast_fusion.2, f32[64,128,256]{2,1,0:T(8,128)S(1)} %fusion.5), kind=kOutput, calls=%fused_computation.42 | convolution fusion | flops 50397184 | bytes 8520192 | tf_op jit(solution)/shard_map/nr,nmh->rmh/dot_general | solution.py:94
  220.5 13.3 %all_gather.17 = bf16[256,1024]{1,0:T(8,128)(2,1)S(1)} all-gather(bf16[256,256]{1,0:T(8,128)(2,1)S(1)} %bitcast.107), channel_id=1, replica_groups=mesh['paper'=64,'author'=4] {'author'}, dimensions={1}, use_global_device_ids=true | all-gather | bytes 655360 | tf_op jit(solution)/shard_map/all_gather | solution.py:131
  233.8 0.4 fusion.40
  234.2 1.4 fusion.25
  235.6 0.4 fusion.43
  236.1 12.8 %all_gather.19 = bf16[256,1024]{0,1:T(8,128)(2,1)S(1)} all-gather(bf16[256,256]{0,1:T(8,128)(2,1)S(1)} %get-tuple-element.20), channel_id=1, replica_groups=mesh['paper'=64,'author'=4] {'author'}, dimensions={1}, use_global_device_ids=true | all-gather | bytes 655360 | tf_op jit(solution)/shard_map/all_gather | solution.py:145
  248.9 0.3 convolution_convert_fusion.2
  249.2 0.0 copy-start.17
  249.2 2.5 gather_fusion.3
  251.8 5.5 %fusion.8 = bf16[48,128,256]{1,2,0:T(8,128)(2,1)} fusion(f32[48]{0:T(128)S(1)} %copy-done.17, bf16[48,128,128]{2,1,0:T(8,128)(2,1)} %param.24, bf16[48,128,256]{2,1,0:T(8,128)(2,1)} %gather_fusion.3, pred[48]{0:T(512)(128)(4,1)S(1)} %copy-done.18), kind=kOutput, calls=%fused_computation.18 | convolution fusion | flops 407371776 | bytes 7864560 | tf_op jit(solution)/shard_map/pdg,pdw->pgw/dot_general | solution.py:156
  257.3 4.9 %copy.105 = bf16[48,128,256]{2,0,1:T(8,128)(2,1)} copy(bf16[48,128,256]{1,2,0:T(8,128)(2,1)} %fusion.8) | data formatting | bytes 6291456 | tf_op jit(solution)/shard_map/convert_element_type | solution.py:159
  262.2 3.2 convert_bitcast_fusion.1
  265.4 4.4 copy.106
  269.8 10.6 %all-to-all-start.3 = ((bf16[64,1,128,256]{3,2,1,0:T(8,128)(2,1)}), bf16[64,1,128,256]{3,2,1,0:T(8,128)(2,1)}, u32[]{:S(2)}, u32[]{:S(2)}) async-start(bf16[64,1,128,256]{3,2,1,0:T(8,128)(2,1)} %copy.106), calls=%async_computation.3 | async-start | bytes 8388608 | tf_op jit(solution)/shard_map/all_to_all | solution.py:169
  280.5 0.3 convolution_convert_fusion.1
  280.8 2.1 gather_fusion.4
  282.9 4.3 fusion.20
  287.2 4.6 copy.110
  291.8 2.9 convert_bitcast_fusion
  294.7 4.4 copy.111
  299.1 77.5 %all-to-all-done.3 = bf16[64,1,128,256]{3,2,1,0:T(8,128)(2,1)} async-done(((bf16[64,1,128,256]{3,2,1,0:T(8,128)(2,1)}), bf16[64,1,128,256]{3,2,1,0:T(8,128)(2,1)}, u32[]{:S(2)}, u32[]{:S(2)}) %all-to-all-start.3) | async-done | bytes 4194336 | tf_op jit(solution)/shard_map/all_to_all | solution.py:169
  376.6 5.7 %all-to-all-start.4 = ((bf16[64,1,128,256]{3,2,1,0:T(8,128)(2,1)}), bf16[64,1,128,256]{3,2,1,0:T(8,128)(2,1)}, u32[]{:S(2)}, u32[]{:S(2)}) async-start(bf16[64,1,128,256]{3,2,1,0:T(8,128)(2,1)} %copy.111), calls=%async_computation.4 | async-start | bytes 8388608 | tf_op jit(solution)/shard_map/all_to_all | solution.py:198
  382.3 2.0 reduce.2
  384.3 0.8 copy.114
  385.1 6.5 %copy.121 = bf16[64,128,256]{1,0,2:T(8,128)(2,1)} copy(bf16[64,128,256]{2,1,0:T(8,128)(2,1)} %bitcast.29) | data formatting | bytes 8388608 | tf_op jit(solution)/shard_map/reshape | solution.py:174
  391.6 2.8 fusion.60
  394.4 1.4 fusion.30
  395.8 0.8 copy.115
  396.6 82.0 %all-to-all-done.4 = bf16[64,1,128,256]{3,2,1,0:T(8,128)(2,1)} async-done(((bf16[64,1,128,256]{3,2,1,0:T(8,128)(2,1)}), bf16[64,1,128,256]{3,2,1,0:T(8,128)(2,1)}, u32[]{:S(2)}, u32[]{:S(2)}) %all-to-all-start.4) | async-done | bytes 4194336 | tf_op jit(solution)/shard_map/all_to_all | solution.py:198
  478.6 4.5 fusion.27
  483.1 0.7 copy.113
  (53 shorter events, 0.2 us)
Async XLA Ops:
  7.2 228.5 %copy-start = (bf16[1024,1024]{1,0:T(8,128)(2,1)S(1)}, bf16[1024,1024]{1,0:T(8,128)(2,1)}, u32[]{:S(2)}) copy-start(bf16[1024,1024]{1,0:T(8,128)(2,1)} %param.32) | copy-start | bytes 6291460
  7.2 25.9 %copy-start.1 = (bf16[256,256]{1,0:T(8,128)(2,1)S(1)}, bf16[256,256]{1,0:T(8,128)(2,1)}, u32[]{:S(2)}) copy-start(bf16[256,256]{1,0:T(8,128)(2,1)} %param.18) | copy-start | bytes 393220
  7.2 193.4 %all-gather.2.cloned.1.call-start = ((), (), s32[]{:S(2)}) async-start(), calls=%async_computation.5 | async-start | bytes 8519680 | tf_op jit(solution)/shard_map/all_gather | solution.py:85
  9.5 0.7 copy-start.6
  40.4 5.9 %copy-start.2 = (bf16[256,256]{1,0:T(8,128)(2,1)S(1)}, bf16[256,256]{1,0:T(8,128)(2,1)}, u32[]{:S(2)}) copy-start(bf16[256,256]{1,0:T(8,128)(2,1)} %param.17) | copy-start | bytes 393220
  40.4 6.7 %copy-start.4 = (bf16[256,256]{1,0:T(8,128)(2,1)S(1)}, bf16[256,256]{1,0:T(8,128)(2,1)}, u32[]{:S(2)}) copy-start(bf16[256,256]{1,0:T(8,128)(2,1)} %param.33) | copy-start | bytes 393220
  40.4 6.8 %copy-start.11 = (s32[48,1]{0,1:T(1,128)S(1)}, s32[48,1]{0,1:T(1,128)}, u32[]{:S(2)}) copy-start(s32[48,1]{0,1:T(1,128)} %param.19) | copy-start | bytes 580
  40.4 7.0 %copy-start.12 = (s32[48]{0:T(128)S(1)}, s32[48]{0:T(128)}, u32[]{:S(2)}) copy-start(s32[48]{0:T(128)} %param.20) | copy-start | bytes 580
  40.4 7.8 %copy-start.10 = (s32[32,1]{0,1:T(1,128)S(1)}, s32[32,1]{0,1:T(1,128)}, u32[]{:S(2)}) copy-start(s32[32,1]{0,1:T(1,128)} %param.25) | copy-start | bytes 388
  40.5 7.8 %copy-start.14 = (s32[48]{0:T(128)S(1)}, s32[48]{0:T(128)}, u32[]{:S(2)}) copy-start(s32[48]{0:T(128)} %param.21) | copy-start | bytes 580
  40.5 7.8 %copy-start.13 = (s32[48]{0:T(128)S(1)}, s32[48]{0:T(128)}, u32[]{:S(2)}) copy-start(s32[48]{0:T(128)} %param.22) | copy-start | bytes 580
  40.5 21.9 %copy-start.15 = (s32[32]{0:T(128)S(1)}, s32[32]{0:T(128)}, u32[]{:S(2)}) copy-start(s32[32]{0:T(128)} %param.28) | copy-start | bytes 388
  40.5 122.1 %all-to-all-start.1 = ((bf16[64,1,128,256]{3,2,1,0:T(8,128)(2,1)}), bf16[64,1,128,256]{3,2,1,0:T(8,128)(2,1)}, u32[]{:S(2)}, u32[]{:S(2)}) async-start(bf16[64,1,128,256]{3,2,1,0:T(8,128)(2,1)} %bitcast_select_fusion), calls=%async_computation.1 | async-start | bytes 8388608 | tf_op jit(solution)/shard_map/all_to_all | solution.py:111
  48.3 0.5 copy-start.16
  62.4 120.0 %copy-start.8 = (f32[32]{0:T(128)}, f32[32]{0:T(128)S(1)}, u32[]{:S(2)}) copy-start(f32[32]{0:T(128)S(1)} %convert_divide_fusion) | copy-start | bytes 388
  162.6 107.2 %all-to-all-start.2 = ((s32[64,1,1]{2,1,0:T(1,128)}), s32[64,1,1]{2,1,0:T(1,128)}, u32[]{:S(2)}, u32[]{:S(2)}) async-start(s32[64,1,1]{2,1,0:T(1,128)} %copy.103), calls=%async_computation.2 | async-start | bytes 65536 | tf_op jit(solution)/shard_map/all_to_all | solution.py:70
  176.9 5.5 %copy-start.5 = (s32[32]{0:T(128)S(1)}, s32[32]{0:T(128)}, u32[]{:S(2)}) copy-start(s32[32]{0:T(128)} %param.26) | copy-start | bytes 388
  211.9 22.0 %copy-start.3 = (bf16[1024,1024]{1,0:T(8,128)(2,1)S(1)}, bf16[1024,1024]{1,0:T(8,128)(2,1)}, u32[]{:S(2)}) copy-start(bf16[1024,1024]{1,0:T(8,128)(2,1)} %param.31) | copy-start | bytes 6291460
  249.2 2.5 copy-start.17
  249.2 2.5 copy-start.18
  269.8 106.8 %all-to-all-start.3 = ((bf16[64,1,128,256]{3,2,1,0:T(8,128)(2,1)}), bf16[64,1,128,256]{3,2,1,0:T(8,128)(2,1)}, u32[]{:S(2)}, u32[]{:S(2)}) async-start(bf16[64,1,128,256]{3,2,1,0:T(8,128)(2,1)} %copy.106), calls=%async_computation.3 | async-start | bytes 8388608 | tf_op jit(solution)/shard_map/all_to_all | solution.py:169
  280.4 2.5 copy-start.9
  287.2 4.6 copy-start.7
  376.6 101.9 %all-to-all-start.4 = ((bf16[64,1,128,256]{3,2,1,0:T(8,128)(2,1)}), bf16[64,1,128,256]{3,2,1,0:T(8,128)(2,1)}, u32[]{:S(2)}, u32[]{:S(2)}) async-start(bf16[64,1,128,256]{3,2,1,0:T(8,128)(2,1)} %copy.111), calls=%async_computation.4 | async-start | bytes 8388608 | tf_op jit(solution)/shard_map/all_to_all | solution.py:198
Sparse Core Ops, SparseCore 0:
  10.8 133.2 all-gather.1
where the time goes:
time: 499 us; the launch traced here: 491 us
  waiting for transfers between devices  256 us (51%)
  blocking collectives  74.6 us (15%)
  matrix products  54.6 us (11%)
  local copies, waits for them, and re-layouts  51.6 us (10%)
  starting transfers between devices  27.5 us (6%)
  between operations  15.3 us (3%)
  other arithmetic  11 us (2%)
    all_to_all x1, waiting for transfers between devices, body(): lax.all_to_all(author_out, 'paper', split_axis=0, concat_axis=0, tiled=True)  96 us
    all_to_all x1, waiting for transfers between devices, body(): lax.all_to_all(author_send, 'paper', split_axis=0, concat_axis=0, tiled=T...  82 us
    all_to_all x1, waiting for transfers between devices, body(): lax.all_to_all(outgoing_grad, 'paper', split_axis=0, concat_axis=0, tiled...  77.5 us
    all_to_all x1, blocking collectives, body(): lax.all_to_all(wanted_authors.reshape(peer_count, wslot_count), 'paper',...  21.5 us
    all_gather x1, blocking collectives, body(): writes = lax.all_gather(authorship_sum, 'author', axis=1, tiled=True)  13.9 us
    all_gather x1, blocking collectives, body(): cites = lax.all_gather(cite_sum, 'author', axis=1, tiled=True)  13.3 us
    all_gather x1, blocking collectives, body(): feats = lax.all_gather(paper_feat, 'author', axis=1, tiled=True)  13 us
    all_gather x1, blocking collectives, body(): pieces = lax.all_gather(grad_pre, 'author', axis=1, tiled=True)  12.8 us
  transfers between devices with their start and end apart: 5, of which 3 were waited for; matrix products, arithmetic and copies ran while one was open for 23% of the time, Pallas kernels for 0%

commit v1 on v0

--- a/solution.py
+++ b/solution.py
@@ -127,7 +127,15 @@
     )
     authorship_sum = authorship_sum.reshape(paper_rows, quarter).astype(jnp.bfloat16)
     column = lax.axis_index("author") * quarter
-    feats = lax.all_gather(paper_feat, "author", axis=1, tiled=True)
+    axis_total = lax.psum(1, "author")
+    sheets = [(j, (j + 1) % axis_total) for j in range(axis_total)]
+    oldest = [None] * axis_total
+    oldest[axis_total - 1] = paper_feat
+    for w in range(axis_total - 2, -1, -1):
+        oldest[w] = lax.ppermute(oldest[w + 1], "author", perm=sheets)
+    tall = jnp.concatenate(oldest, 1)
+    before = lax.axis_index("author")
+    feats = jnp.roll(tall, (before + 1) * paper_feat.shape[1], 1)
     cites = lax.all_gather(cite_sum, "author", axis=1, tiled=True)
     writes = lax.all_gather(authorship_sum, "author", axis=1, tiled=True)
     span = feats.shape[1]

time: 499 us -> 511 us (1.024)
  starting transfers between devices: 27.5 us -> 42.6 us
  blocking collectives: 74.6 us -> 61 us
  waiting for transfers between devices: 256 us -> 263 us
    all_gather x1 -> x0, blocking collectives: 13 us -> none  [body(): feats = lax.all_gather(paper_feat, 'author', axis=1, tiled=True)]
    all_to_all x1, starting transfers between devices: 5.42 us -> 16.1 us  [body(): lax.all_to_all(wanted.reshape(peer_count, slot_count), 'paper', split_axi...]
    all_to_all x1, waiting for transfers between devices: 82 us -> 89.4 us  [body(): lax.all_to_all(author_send, 'paper', split_axis=0, concat_axis=0, tiled=T...]
    reshape x1 -> x0, local copies, waits for them, and re-layouts: 6.54 us -> none  [body(): arrived.reshape(slot_total, tile_rows, quarter)]
    all_to_all x1, waiting for transfers between devices: 96 us -> 89.9 us  [body(): lax.all_to_all(author_out, 'paper', split_axis=0, concat_axis=0, tiled=True)]
    ppermute x0 -> x3, waiting for transfers between devices: none -> 6.09 us  [body(): oldest[w] = lax.ppermute(oldest[w + 1], 'author', perm=sheets)]
  transfers between devices with their start and end apart: 5 -> 8, of which waited for: 3 -> 5; matrix products, arithmetic and copies ran while one was open for 23% -> 23% of each run, Pallas kernels for 0% -> 0%
where the time goes in v1:
time: 511 us; the launch traced here: 503 us
  waiting for transfers between devices  263 us (51%)
  blocking collectives  61 us (12%)
  matrix products  59 us (12%)
  local copies, waits for them, and re-layouts  50.3 us (10%)
  starting transfers between devices  42.6 us (8%)
  between operations  15.5 us (3%)
  other arithmetic  11.9 us (2%)
    all_to_all x1, waiting for transfers between devices, body(): lax.all_to_all(author_out, 'paper', split_axis=0, concat_axis=0, tiled=True)  89.9 us
    all_to_all x1, waiting for transfers between devices, body(): lax.all_to_all(author_send, 'paper', split_axis=0, concat_axis=0, tiled=T...  89.4 us
    all_to_all x1, waiting for transfers between devices, body(): lax.all_to_all(outgoing_grad, 'paper', split_axis=0, concat_axis=0, tiled...  76.6 us
    all_to_all x1, blocking collectives, body(): lax.all_to_all(wanted_authors.reshape(peer_count, wslot_count), 'paper',...  21.5 us
    all_to_all x1, starting transfers between devices, body(): lax.all_to_all(wanted.reshape(peer_count, slot_count), 'paper', split_axi...  16.1 us
    all_gather x1, blocking collectives, body(): writes = lax.all_gather(authorship_sum, 'author', axis=1, tiled=True)  13.4 us
    all_gather x1, blocking collectives, body(): cites = lax.all_gather(cite_sum, 'author', axis=1, tiled=True)  13.4 us
    all_gather x1, blocking collectives, body(): pieces = lax.all_gather(grad_pre, 'author', axis=1, tiled=True)  12.8 us
  transfers between devices with their start and end apart: 8, of which 5 were waited for; matrix products, arithmetic and copies ran while one was open for 23% of the time, Pallas kernels for 0%

profile of v1, /device:TPU:2, one launch (start us, length us, event | category | flops | bytes accessed | tf_op | source)
XLA Modules:
  0.0 503.1 jit_solution(9873591713581740130)
XLA Ops:
  7.2 0.7 all-gather.2.cloned.1.call-update
  7.9 0.9 convert_reduce_fusion.1
  8.8 0.7 fusion.87
  9.5 0.7 select_reduce_fusion.1
  10.3 21.5 %all_to_all.39 = s32[64,1,1]{2,1,0:T(1,128)S(1)} all-to-all(s32[64,1,1]{2,1,0:T(1,128)S(1)} %copy.66), channel_id=1, replica_groups=mesh['paper'=64,'author'=4] {'paper'}, dimensions={0} | all-to-all | bytes 512 | tf_op jit(solution)/shard_map/all_to_all | solution.py:100
  31.8 1.2 reduce
  33.1 2.8 gather_fusion.1
  35.9 4.6 bitcast_select_fusion
  40.5 5.8 %all-to-all-start.1 = ((bf16[64,1,128,256]{3,2,1,0:T(8,128)(2,1)}), bf16[64,1,128,256]{3,2,1,0:T(8,128)(2,1)}, u32[]{:S(2)}, u32[]{:S(2)}) async-start(bf16[64,1,128,256]{3,2,1,0:T(8,128)(2,1)} %bitcast_select_fusion), calls=%async_computation.1 | async-start | bytes 8388608 | tf_op jit(solution)/shard_map/all_to_all | solution.py:111
  46.3 1.6 collective-permute-start
  48.9 0.5 compare_and_fusion.3
  49.4 0.6 compare_and_fusion.1
  50.0 0.6 convert_divide_fusion
  50.6 0.5 and_bitcast_fusion
  51.1 4.2 convolution_convert_fusion
  55.4 1.3 collective-permute-start.1
  56.7 3.8 collective-permute-done.1
  60.4 1.2 collective-permute-start.2
  61.6 0.7 copy.70
  62.3 0.8 convolution_bitcast_fusion.1
  63.2 2.3 collective-permute-done.2
  65.5 1.6 constant_dynamic-update-slice_fusion.7
  67.1 0.7 constant_dynamic-update-slice_fusion.6
  67.8 0.7 constant_dynamic-update-slice_fusion.5
  68.4 0.7 constant_dynamic-update-slice_fusion.4
  69.1 1.6 constant_dynamic-update-slice_fusion.3
  70.7 0.7 constant_dynamic-update-slice_fusion.2
  71.4 0.7 constant_dynamic-update-slice_fusion.1
  72.1 0.7 constant_dynamic-update-slice_fusion
  72.8 89.9 %all-to-all-done.1 = bf16[64,1,128,256]{3,2,1,0:T(8,128)(2,1)} async-done(((bf16[64,1,128,256]{3,2,1,0:T(8,128)(2,1)}), bf16[64,1,128,256]{3,2,1,0:T(8,128)(2,1)}, u32[]{:S(2)}, u32[]{:S(2)}) %all-to-all-start.1) | async-done | bytes 4194336 | tf_op jit(solution)/shard_map/all_to_all | solution.py:111
  162.6 16.1 %all-to-all-start.2 = ((s32[64,1,1]{2,1,0:T(1,128)}), s32[64,1,1]{2,1,0:T(1,128)S(1)}, u32[]{:S(2)}, u32[]{:S(2)}) async-start(s32[64,1,1]{2,1,0:T(1,128)} %copy.70), calls=%async_computation.2 | async-start | bytes 65536 | tf_op jit(solution)/shard_map/all_to_all | solution.py:70
  178.8 4.2 gather_fusion.2
  183.0 4.4 convolution_bitcast_fusion
  187.4 5.5 %copy.68 = f32[32,128,256]{2,0,1:T(8,128)} copy(f32[32,128,256]{1,2,0:T(8,128)} %convolution_bitcast_fusion) | data formatting | bytes 8388608 | tf_op jit(solution)/shard_map/eih,ehp->eip/dot_general | solution.py:116
  192.9 4.3 convolution_convert_fusion.3
  197.2 13.4 %all_gather.14 = bf16[256,1024]{1,0:T(8,128)(2,1)S(1)} all-gather(bf16[256,256]{1,0:T(8,128)(2,1)S(1)} %bitcast.98), channel_id=1, replica_groups=mesh['paper'=64,'author'=4] {'author'}, dimensions={1}, use_global_device_ids=true | all-gather | bytes 655360 | tf_op jit(solution)/shard_map/all_gather | solution.py:140
  210.6 1.3 fusion.42
  212.0 6.2 %gather_fusion = bf16[64,128,256]{2,1,0:T(8,128)(2,1)} fusion(bf16[128,128,256]{2,1,0:T(8,128)(2,1)} %bitcast.96, s32[1024]{0:T(1024)S(1)} %pad_clamp_fusion.4), kind=kCustom, calls=%fused_computation | custom fusion | bytes 8388864 | tf_op jit(solution)/shard_map/jit(_take)/gather | solution.py:90
  218.1 5.1 %fusion.8 = f32[64,128,256]{2,1,0:T(8,128)S(1)} fusion(bf16[64,128,256]{2,1,0:T(8,128)(2,1)} %gather_fusion, pred[64]{0:T(512)(128)(4,1)S(1)} %copy-done.13, bf16[64,128,128]{2,0,1:T(8,128)(2,1)} %convolution_convert_fusion), kind=kOutput, calls=%fused_computation.18 | convolution fusion | flops 538968064 | bytes 14680128 | tf_op jit(solution)/shard_map/eih,ehp->eip/dot_general | solution.py:91
  223.2 8.6 %fusion.34 = bf16[2,128,256]{2,0,1:T(2,128)(2,1)S(1)} fusion(f32[64,2,1]{0,1,2:T(2,128)S(1)} %copy-done.8, f32[64,128,256]{2,1,0:T(8,128)S(1)} %fusion.8), kind=kOutput, calls=%fused_computation.44 | convolution fusion | flops 50397184 | bytes 8520192 | tf_op jit(solution)/shard_map/nr,nmh->rmh/dot_general | solution.py:94
  231.9 13.4 %all_gather.13 = bf16[256,1024]{1,0:T(8,128)(2,1)S(1)} all-gather(bf16[256,256]{1,0:T(8,128)(2,1)S(1)} %bitcast.99), channel_id=1, replica_groups=mesh['paper'=64,'author'=4] {'author'}, dimensions={1}, use_global_device_ids=true | all-gather | bytes 655360 | tf_op jit(solution)/shard_map/all_gather | solution.py:139
  245.6 2.1 fusion.48
  247.7 12.8 %all_gather.15 = bf16[256,1024]{1,0:T(8,128)(2,1)S(1)} all-gather(bf16[256,256]{1,0:T(8,128)(2,1)S(1)} %get-tuple-element.5), channel_id=1, replica_groups=mesh['paper'=64,'author'=4] {'author'}, dimensions={1}, use_global_device_ids=true | all-gather | bytes 655360 | tf_op jit(solution)/shard_map/all_gather | solution.py:153
  260.4 0.3 convolution_convert_fusion.2
  260.8 2.5 gather_fusion.3
  263.3 5.6 %fusion.11 = bf16[48,128,256]{1,2,0:T(8,128)(2,1)} fusion(f32[48]{0:T(128)S(1)} %copy-done.21, bf16[48,128,128]{2,1,0:T(8,128)(2,1)} %param.24, bf16[48,128,256]{2,1,0:T(8,128)(2,1)} %gather_fusion.3, pred[48]{0:T(512)(128)(4,1)S(1)} %copy-done.22), kind=kOutput, calls=%fused_computation.21 | convolution fusion | flops 407371776 | bytes 7864560 | tf_op jit(solution)/shard_map/pdg,pdw->pgw/dot_general | solution.py:164
  268.9 5.0 copy.72
  273.9 3.2 convert_bitcast_fusion.1
  277.1 4.4 copy.73
  281.5 10.6 %all-to-all-start.3 = ((bf16[64,1,128,256]{3,2,1,0:T(8,128)(2,1)}), bf16[64,1,128,256]{3,2,1,0:T(8,128)(2,1)}, u32[]{:S(2)}, u32[]{:S(2)}) async-start(bf16[64,1,128,256]{3,2,1,0:T(8,128)(2,1)} %copy.73), calls=%async_computation.3 | async-start | bytes 8388608 | tf_op jit(solution)/shard_map/all_to_all | solution.py:177
  292.2 1.4 convolution_convert_fusion.1
  293.6 2.0 gather_fusion.4
  295.6 4.3 fusion.23
  299.9 4.5 copy.77
  304.4 2.9 convert_bitcast_fusion
  307.4 4.4 copy.78
  311.8 76.6 %all-to-all-done.3 = bf16[64,1,128,256]{3,2,1,0:T(8,128)(2,1)} async-done(((bf16[64,1,128,256]{3,2,1,0:T(8,128)(2,1)}), bf16[64,1,128,256]{3,2,1,0:T(8,128)(2,1)}, u32[]{:S(2)}, u32[]{:S(2)}) %all-to-all-start.3) | async-done | bytes 4194336 | tf_op jit(solution)/shard_map/all_to_all | solution.py:177
  388.4 5.9 %all-to-all-start.4 = ((bf16[64,1,128,256]{3,2,1,0:T(8,128)(2,1)}), bf16[64,1,128,256]{3,2,1,0:T(8,128)(2,1)}, u32[]{:S(2)}, u32[]{:S(2)}) async-start(bf16[64,1,128,256]{3,2,1,0:T(8,128)(2,1)} %copy.78), calls=%async_computation.4 | async-start | bytes 8388608 | tf_op jit(solution)/shard_map/all_to_all | solution.py:206
  394.3 1.2 reduce.2
  395.5 4.5 fusion.4
  400.1 1.0 fusion.33
  401.1 89.4 %all-to-all-done.4 = bf16[64,1,128,256]{3,2,1,0:T(8,128)(2,1)} async-done(((bf16[64,1,128,256]{3,2,1,0:T(8,128)(2,1)}), bf16[64,1,128,256]{3,2,1,0:T(8,128)(2,1)}, u32[]{:S(2)}, u32[]{:S(2)}) %all-to-all-start.4) | async-done | bytes 4194336 | tf_op jit(solution)/shard_map/all_to_all | solution.py:206
  490.5 4.5 fusion.30
  495.1 0.7 copy.80
  (70 shorter events, 1.0 us)
Async XLA Ops:
  7.2 238.4 %copy-start = (bf16[1024,1024]{1,0:T(8,128)(2,1)S(1)}, bf16[1024,1024]{1,0:T(8,128)(2,1)}, u32[]{:S(2)}) copy-start(bf16[1024,1024]{1,0:T(8,128)(2,1)} %param.30) | copy-start | bytes 6291460
  7.2 25.9 %copy-start.1 = (bf16[256,256]{1,0:T(8,128)(2,1)S(1)}, bf16[256,256]{1,0:T(8,128)(2,1)}, u32[]{:S(2)}) copy-start(bf16[256,256]{1,0:T(8,128)(2,1)} %param.18) | copy-start | bytes 393220
  7.2 204.8 %all-gather.2.cloned.1.call-start = ((), (), s32[]{:S(2)}) async-start(), calls=%async_computation.5 | async-start | bytes 8519680 | tf_op jit(solution)/shard_map/all_gather | solution.py:85
  9.5 0.7 copy-start.10
  40.5 5.9 %copy-start.2 = (bf16[256,256]{1,0:T(8,128)(2,1)S(1)}, bf16[256,256]{1,0:T(8,128)(2,1)}, u32[]{:S(2)}) copy-start(bf16[256,256]{1,0:T(8,128)(2,1)} %param.17) | copy-start | bytes 393220
  40.5 8.1 %copy-start.15 = (s32[48,1]{0,1:T(1,128)S(1)}, s32[48,1]{0,1:T(1,128)}, u32[]{:S(2)}) copy-start(s32[48,1]{0,1:T(1,128)} %param.19) | copy-start | bytes 580
  40.5 8.3 %copy-start.16 = (s32[48]{0:T(128)S(1)}, s32[48]{0:T(128)}, u32[]{:S(2)}) copy-start(s32[48]{0:T(128)} %param.20) | copy-start | bytes 580
  40.5 8.9 %copy-start.19 = (s32[48]{0:T(128)S(1)}, s32[48]{0:T(128)}, u32[]{:S(2)}) copy-start(s32[48]{0:T(128)} %param.21) | copy-start | bytes 580
  40.5 9.5 %copy-start.17 = (s32[32]{0:T(128)S(1)}, s32[32]{0:T(128)}, u32[]{:S(2)}) copy-start(s32[32]{0:T(128)} %param.28) | copy-start | bytes 388
  40.5 10.1 %copy-start.14 = (s32[32,1]{0,1:T(1,128)S(1)}, s32[32,1]{0,1:T(1,128)}, u32[]{:S(2)}) copy-start(s32[32,1]{0,1:T(1,128)} %param.25) | copy-start | bytes 388
  40.5 122.1 %all-to-all-start.1 = ((bf16[64,1,128,256]{3,2,1,0:T(8,128)(2,1)}), bf16[64,1,128,256]{3,2,1,0:T(8,128)(2,1)}, u32[]{:S(2)}, u32[]{:S(2)}) async-start(bf16[64,1,128,256]{3,2,1,0:T(8,128)(2,1)} %bitcast_select_fusion), calls=%async_computation.1 | async-start | bytes 8388608 | tf_op jit(solution)/shard_map/all_to_all | solution.py:111
  46.3 9.0 %copy-start.18 = (s32[48]{0:T(128)S(1)}, s32[48]{0:T(128)}, u32[]{:S(2)}) copy-start(s32[48]{0:T(128)} %param.22) | copy-start | bytes 580
  46.3 9.0 %collective-permute-start = (bf16[256,256]{1,0:T(8,128)(2,1)S(1)}, bf16[256,256]{1,0:T(8,128)(2,1)S(1)}, u32[]{:S(2)}, u32[]{:S(2)}) collective-permute-start(bf16[256,256]{1,0:T(8,128)(2,1)S(1)} %copy-done.2), channel_id=1, source_target_pairs={{0,1},{1,2},{2,3},{3,0},{4,5},{5,6},{6,7},{7,4},{8,9},{9,10},{10,1... | collective-permute-start | bytes 393224 | tf_op jit(solution)/shard_map/ppermute | solution.py:135
  48.8 13.6 %copy-start.6 = (s32[48]{0:T(128)}, s32[48]{0:T(128)S(1)}, u32[]{:S(2)}) copy-start(s32[48]{0:T(128)S(1)} %fusion.81) | copy-start | bytes 580
  55.3 7.0 %copy-start.20 = (f32[48]{0:T(128)}, f32[48]{0:T(128)S(1)}, u32[]{:S(2)}) copy-start(f32[48]{0:T(128)S(1)} %compare_select_fusion.8) | copy-start | bytes 580
  55.4 5.1 %collective-permute-start.1 = (bf16[256,256]{1,0:T(8,128)(2,1)S(1)}, bf16[256,256]{1,0:T(8,128)(2,1)S(1)}, u32[]{:S(2)}, u32[]{:S(2)}) collective-permute-start(bf16[256,256]{1,0:T(8,128)(2,1)S(1)} %collective-permute-done), channel_id=1, source_target_pairs={{0,1},{1,2},{2,3},{3,0},{4,5},{5,6},{6,7},{7,4},{8,9},{9,10},{10,1... | collective-permute-start | bytes 393224 | tf_op jit(solution)/shard_map/ppermute | solution.py:135
  60.4 5.1 %collective-permute-start.2 = (bf16[256,256]{1,0:T(8,128)(2,1)S(1)}, bf16[256,256]{1,0:T(8,128)(2,1)}, u32[]{:S(2)}, u32[]{:S(2)}) collective-permute-start(bf16[256,256]{1,0:T(8,128)(2,1)S(1)} %collective-permute-done.1), channel_id=1, source_target_pairs={{0,1},{1,2},{2,3},{3,0},{4,5},{5,6},{6,7},{7,4},{8,9},{9,10},{10,1... | collective-permute-start | bytes 393224 | tf_op jit(solution)/shard_map/ppermute | solution.py:135
  63.2 119.8 %copy-start.3 = (bf16[32,128,128]{2,1,0:T(8,128)(2,1)S(1)}, bf16[32,128,128]{2,1,0:T(8,128)(2,1)}, u32[]{:S(2)}) copy-start(bf16[32,128,128]{2,1,0:T(8,128)(2,1)} %param.29) | copy-start | bytes 3145732
  162.6 118.9 %all-to-all-start.2 = ((s32[64,1,1]{2,1,0:T(1,128)}), s32[64,1,1]{2,1,0:T(1,128)S(1)}, u32[]{:S(2)}, u32[]{:S(2)}) async-start(s32[64,1,1]{2,1,0:T(1,128)} %copy.70), calls=%async_computation.2 | async-start | bytes 65536 | tf_op jit(solution)/shard_map/all_to_all | solution.py:70
  187.4 5.5 %copy-start.9 = (s32[32]{0:T(128)S(1)}, s32[32]{0:T(128)}, u32[]{:S(2)}) copy-start(s32[32]{0:T(128)} %param.26) | copy-start | bytes 388
  187.4 5.5 %copy-start.12 = (f32[32]{0:T(128)S(1)}, f32[32]{0:T(128)}, u32[]{:S(2)}) copy-start(f32[32]{0:T(128)} %convert_divide_fusion) | copy-start | bytes 388
  212.0 6.2 %copy-start.13 = (pred[64]{0:T(512)(128)(4,1)S(1)}, pred[64]{0:T(512)(128)(4,1)}, u32[]{:S(2)}) copy-start(pred[64]{0:T(512)(128)(4,1)} %compare_and_fusion.3) | copy-start | bytes 196
  218.1 5.1 %copy-start.8 = (f32[64,2,1]{0,1,2:T(2,128)S(1)}, f32[64,2,1]{0,1,2:T(2,128)}, u32[]{:S(2)}) copy-start(f32[64,2,1]{0,1,2:T(2,128)} %convolution_bitcast_fusion.1) | copy-start | bytes 1540
  223.2 22.0 %copy-start.4 = (bf16[1024,1024]{1,0:T(8,128)(2,1)S(1)}, bf16[1024,1024]{1,0:T(8,128)(2,1)}, u32[]{:S(2)}) copy-start(bf16[1024,1024]{1,0:T(8,128)(2,1)} %param.31) | copy-start | bytes 6291460
  223.2 22.3 %copy-start.5 = (bf16[256,256]{1,0:T(8,128)(2,1)S(1)}, bf16[256,256]{1,0:T(8,128)(2,1)}, u32[]{:S(2)}) copy-start(bf16[256,256]{1,0:T(8,128)(2,1)} %param.33) | copy-start | bytes 393220
  260.8 2.5 copy-start.21
  260.8 2.5 copy-start.22
  268.9 5.0 copy-start.7
  281.5 106.8 %all-to-all-start.3 = ((bf16[64,1,128,256]{3,2,1,0:T(8,128)(2,1)}), bf16[64,1,128,256]{3,2,1,0:T(8,128)(2,1)}, u32[]{:S(2)}, u32[]{:S(2)}) async-start(bf16[64,1,128,256]{3,2,1,0:T(8,128)(2,1)} %copy.73), calls=%async_computation.3 | async-start | bytes 8388608 | tf_op jit(solution)/shard_map/all_to_all | solution.py:177
  299.9 4.5 copy-start.11
  388.4 102.2 %all-to-all-start.4 = ((bf16[64,1,128,256]{3,2,1,0:T(8,128)(2,1)}), bf16[64,1,128,256]{3,2,1,0:T(8,128)(2,1)}, u32[]{:S(2)}, u32[]{:S(2)}) async-start(bf16[64,1,128,256]{3,2,1,0:T(8,128)(2,1)} %copy.78), calls=%async_computation.4 | async-start | bytes 8388608 | tf_op jit(solution)/shard_map/all_to_all | solution.py:206
Sparse Core Ops, SparseCore 0:
  10.8 133.2 all-gather.1
